TPU v7x, 32 devices: a whole 2x2x4 slice. The times are simulated.
32 devices in a mesh: leaf: 8 (over z, core), bond: 4 (over y, x).
Axes of the slice: x: 2, y: 2, z: 4, core: 2. Of those that a mesh axis runs over, the one named last changes fastest.
Arguments:
- isometries: bfloat16 [8, 256, 256, 256], P('leaf', 'bond'), may hold values from -0.1875 to 0.1875
- leaf_ops: bfloat16 [8, 1, 256, 256], P('leaf', None, 'bond'), may hold values from -6 to 6
- charges: int32 [8, 3, 4], P('leaf'), may hold values from 0 to 3
- assign: int32 [8, 1], P('leaf'), may hold values from 0 to 2
Outputs:
- node_ops: bfloat16 [8, 1, 256, 256], P('leaf', None, 'bond')
Inputs may be any that keep to these rules, and one draw needn't show every extreme that they name: `assign`: 0 takes the left child's operator, 1 the right child's, 2 their sum.
All inputs are finite; a program needn't handle non-finite values.
Results may differ from a plain program's by a relative error of at most 0.008.
Values may be sent and summed in bfloat16 or wider, within the bound.
No kernel may reach another device: no remote copies, remote signals or barrier semaphores. Data moves between devices by JAX's collectives and lax.ppermute only.
A program may use at most 128 MiB of HBM per device.

v0:
```python
import jax
import jax.numpy as jnp
from jax import lax
from jax.sharding import PartitionSpec as P

BLOCK = 64
QMOD = 4
LEVELS = 3


def passed_along(array, axis, by):
    devices = lax.axis_size(axis)
    return lax.ppermute(array, axis, [(i, (i + by) % devices) for i in range(devices)])


def lookup(index_vector, charge_table, blocks):
    hits = index_vector[:, None] == blocks[None, :]
    return jnp.sum(jnp.where(hits, charge_table[None, :], 0), axis=1)


def shards(isometries, leaf_ops, charges, assign):
    bond_rank = lax.axis_index("bond")
    weight = isometries[0]
    slab_rows = weight.shape[0]
    bond_width = weight.shape[1]
    op_count = leaf_ops.shape[1]
    charge_row = charges[0]
    blocks = jnp.arange(charge_row.shape[1], dtype=jnp.int32)
    left_index = (bond_rank * slab_rows + jnp.arange(slab_rows, dtype=jnp.int32)) // BLOCK
    full_index = jnp.arange(bond_width, dtype=jnp.int32) // BLOCK
    charge_left = lookup(left_index, charge_row[0], blocks)
    charge_right = lookup(full_index, charge_row[1], blocks)
    charge_parent = lookup(full_index, charge_row[2], blocks)
    charge_sum = (
        charge_left[:, None, None] + charge_right[None, :, None] - charge_parent[None, None, :]
    )
    keep_mask = jnp.mod(charge_sum, QMOD) == 0
    masked = jnp.where(keep_mask, weight, jnp.zeros((), weight.dtype))
    by_right = lax.all_to_all(masked, "bond", split_axis=1, concat_axis=0, tiled=True)
    take_left = (assign[0] != 1).astype(jnp.float32)
    take_right = (assign[0] != 0).astype(jnp.float32)
    held_ops = lax.all_gather(leaf_ops[0], "bond", axis=1, tiled=True)
    for level_now in range(1, LEVELS + 1):
        reach_by = 2 ** (level_now - 1)
        left_ops = passed_along(held_ops, "leaf", reach_by)
        left_mixed = jnp.dot(
            left_ops.reshape(op_count * bond_width, bond_width),
            by_right.reshape(bond_width, -1),
            preferred_element_type=jnp.float32,
        ).astype(jnp.bfloat16)
        left_mixed = left_mixed.reshape(op_count, -1, bond_width)
        left_part = jnp.einsum(
            "rp,krq->kpq",
            by_right.reshape(-1, bond_width),
            left_mixed,
            preferred_element_type=jnp.float32,
        )
        right_mixed = jnp.einsum(
            "kcb,abq->kacq", held_ops, masked, preferred_element_type=jnp.float32
        ).astype(jnp.bfloat16)
        right_part = jnp.einsum(
            "acp,kacq->kpq", masked, right_mixed, preferred_element_type=jnp.float32
        )
        partial_sum = take_left[:, None, None] * left_part + take_right[:, None, None] * right_part
        held_ops = lax.psum(partial_sum, "bond").astype(jnp.bfloat16)
    result = lax.dynamic_slice_in_dim(held_ops, bond_rank * slab_rows, slab_rows, 1)
    return result[None]


def solution(mesh):
    in_specs = (
        P("leaf", "bond", None, None),
        P("leaf", None, "bond", None),
        P("leaf", None, None),
        P("leaf", None),
    )
    out_specs = P("leaf", None, "bond", None)
    return jax.shard_map(shards, mesh=mesh, in_specs=in_specs, out_specs=out_specs, check_vma=False)
```

profile of v0, /device:TPU:0, one launch (start us, length us, event | category | flops | bytes accessed | tf_op | source)
XLA Modules:
  0.0 373.3 jit_solution(8622077636349442603)
XLA Ops:
  0.0 0.7 slice_bitcast_fusion.2
  0.7 0.1 select_reduce_fusion.2
  0.8 0.1 select_reduce_fusion.1
  0.9 0.1 broadcast_add_fusion
  1.0 0.1 copy.50
  1.1 24.5 %fusion.6 = bf16[64,256,256]{2,0,1:T(8,128)(2,1)} fusion(bf16[1,64,256,256]{3,2,1,0:T(8,128)(2,1)} %param.4, s32[256]{0:T(256)S(1)} %get-tuple-element.6, s32[64,256]{0,1:T(8,128)S(1)} %copy.50), kind=kLoop, calls=%fused_computation.19 | loop fusion | flops 58720256 | bytes 16843776 | tf_op jit(solution)/shard_map/jit(_where)/select_n | solution.py:38
  25.5 5.8 %all-to-all-start = ((bf16[64,256,256]{2,0,1:T(8,128)(2,1)}), bf16[64,256,256]{2,0,1:T(8,128)(2,1)}, u32[]{:S(2)}, u32[]{:S(2)}) async-start(bf16[64,256,256]{2,0,1:T(8,128)(2,1)} %fusion.6), calls=%async_computation | async-start | bytes 16777216 | tf_op jit(solution)/shard_map/all_to_all | solution.py:39
  31.3 97.5 %all-gather = bf16[1,1,256,256]{3,2,1,0:T(8,128)(2,1)S(1)} all-gather(bf16[1,1,64,256]{3,2,1,0:T(8,128)(2,1)S(1)} %copy-done), channel_id=2, replica_groups=mesh['leaf'=8,'bond'=4] {'bond'}, dimensions={2}, use_global_device_ids=true | all-gather | bytes 163840 | tf_op jit(solution)/shard_map/all_gather | solution.py:42
  128.8 0.0 collective-permute-start
  129.5 11.7 %fusion.7 = bf16[64,256,256]{2,1,0:T(8,128)(2,1)} fusion(bf16[1,64,256,256]{3,2,1,0:T(8,128)(2,1)} %param.4, s32[256]{0:T(256)S(1)} %get-tuple-element.6, s32[64,256]{1,0:T(8,128)S(1)} %broadcast_add_fusion), kind=kLoop, calls=%fused_computation.20 | loop fusion | flops 58720256 | bytes 16843776 | tf_op jit(solution)/shard_map/jit(_where)/select_n | solution.py:38
  141.2 10.4 %fusion.26 = f32[256,256]{1,0:T(8,128)S(1)} fusion(bf16[64,256,256]{2,1,0:T(8,128)(2,1)} %fusion.7, bf16[1,1,256,256]{3,2,1,0:T(8,128)(2,1)S(1)} %all-gather, f32[]{:T(128)} %bitcast.14), kind=kOutput, calls=%fused_computation.34 | convolution fusion | flops 4299227136 | bytes 8781828 | tf_op jit(solution)/shard_map/acp,kacq->kpq/dot_general | solution.py:61
  151.7 11.5 %copy.53 = bf16[4,64,64,256]{3,2,1,0:T(8,128)(2,1)} copy(bf16[4,64,64,256]{3,1,2,0:T(8,128)(2,1)} %bitcast.7) | data formatting | bytes 16777216 | tf_op jit(solution)/shard_map/all_to_all | solution.py:39
  163.1 15.4 %copy.71 = bf16[32,8,64,256]{3,1,2,0:T(8,128)(2,1)} copy(bf16[32,8,64,256]{3,2,1,0:T(8,128)(2,1)} %bitcast.124) | data formatting | bytes 16777216
  178.6 9.0 %fusion = bf16[256,16384]{0,1:T(8,128)(2,1)} fusion(bf16[256,16384]{1,0:T(8,128)(2,1)} %bitcast.128, bf16[1,256,256]{2,1,0:T(8,128)(2,1)S(1)} %collective-permute-done), kind=kOutput, calls=%fused_computation.13 | convolution fusion | flops 2151677952 | bytes 16908288 | tf_op jit(solution)/shard_map/dot_general | solution.py:46
  187.5 12.0 %copy.54 = bf16[256,16384]{1,0:T(8,128)(2,1)} copy(bf16[256,16384]{0,1:T(8,128)(2,1)} %fusion) | data formatting | bytes 16777216 | tf_op jit(solution)/shard_map/convert_element_type | solution.py:50
  199.5 13.6 %reshape.215 = bf16[16384,256]{1,0:T(8,128)(2,1)} reshape(bf16[256,16384]{1,0:T(8,128)(2,1)} %copy.54) | data formatting | bytes 16777216 | tf_op jit(solution)/shard_map/reshape.9
  213.2 8.1 %fusion.42 = f32[1,256,256]{1,2,0:T(8,128)S(1)} fusion(f32[256,256]{1,0:T(8,128)S(1)} %fusion.26, bf16[16384,256]{1,0:T(8,128)(2,1)} %reshape.215, bf16[16384,256]{1,0:T(8,128)(2,1)} %bitcast.125, f32[]{:T(128)} %bitcast), kind=kOutput, calls=%fused_computation.43 | convolution fusion | flops 2147614720 | bytes 17301508 | tf_op jit(solution)/shard_map/rp,krq->kpq/dot_general | solution.py:52
  221.3 21.3 %all-reduce.3 = bf16[1,256,256]{1,2,0:T(8,128)(2,1)S(1)} all-reduce(f32[1,256,256]{1,2,0:T(8,128)S(1)} %fusion.42), channel_id=1, replica_groups=mesh['leaf'=8,'bond'=4] {'bond'}, use_global_device_ids=true, to_apply=%region_3.4 | all-reduce | flops 65536 | bytes 393216 | tf_op jit(solution)/shard_map/psum | solution.py:65
  242.6 1.7 collective-permute-start.1
  244.3 12.7 %fusion.32 = f32[256,256]{1,0:T(8,128)S(1)} fusion(bf16[64,256,256]{2,1,0:T(8,128)(2,1)} %fusion.7, bf16[1,256,256]{1,2,0:T(8,128)(2,1)S(1)} %all-reduce.3, f32[]{:T(128)} %bitcast.14), kind=kOutput, calls=%fused_computation.36 | convolution fusion | flops 4299227136 | bytes 8781828 | tf_op jit(solution)/shard_map/acp,kacq->kpq/dot_general | solution.py:61
  257.0 9.0 %convolution_convert_fusion.2 = bf16[256,16384]{1,0:T(8,128)(2,1)} fusion(bf16[256,16384]{1,0:T(8,128)(2,1)} %bitcast.129, bf16[1,256,256]{1,2,0:T(8,128)(2,1)S(1)} %collective-permute-done.1), kind=kOutput, calls=%fused_computation.12 | convolution fusion | flops 2151677952 | bytes 16908288 | tf_op jit(solution)/shard_map/dot_general | solution.py:46
  266.0 13.5 %reshape.220 = bf16[16384,256]{1,0:T(8,128)(2,1)} reshape(bf16[256,16384]{1,0:T(8,128)(2,1)} %convolution_convert_fusion.2) | data formatting | bytes 16777216 | tf_op jit(solution)/shard_map/reshape.28
  279.5 8.1 %fusion.44 = f32[1,256,256]{1,2,0:T(8,128)S(1)} fusion(f32[256,256]{1,0:T(8,128)S(1)} %fusion.32, bf16[16384,256]{1,0:T(8,128)(2,1)} %reshape.220, bf16[16384,256]{1,0:T(8,128)(2,1)} %bitcast.126, f32[]{:T(128)} %bitcast), kind=kOutput, calls=%fused_computation.45 | convolution fusion | flops 2147614720 | bytes 17301508 | tf_op jit(solution)/shard_map/rp,krq->kpq/dot_general | solution.py:52
  287.6 19.4 %all-reduce.4 = bf16[1,256,256]{1,2,0:T(8,128)(2,1)S(1)} all-reduce(f32[1,256,256]{1,2,0:T(8,128)S(1)} %fusion.44), channel_id=1, replica_groups=mesh['leaf'=8,'bond'=4] {'bond'}, use_global_device_ids=true, to_apply=%region_4.5 | all-reduce | flops 65536 | bytes 393216 | tf_op jit(solution)/shard_map/psum | solution.py:65
  307.0 1.6 collective-permute-start.2
  308.6 12.7 %fusion.38 = f32[256,256]{1,0:T(8,128)S(1)} fusion(bf16[64,256,256]{2,1,0:T(8,128)(2,1)} %fusion.7, bf16[1,256,256]{1,2,0:T(8,128)(2,1)S(1)} %all-reduce.4, f32[]{:T(128)} %bitcast.14), kind=kOutput, calls=%fused_computation.38 | convolution fusion | flops 4299227136 | bytes 8781828 | tf_op jit(solution)/shard_map/acp,kacq->kpq/dot_general | solution.py:61
  321.4 9.0 %convolution_convert_fusion.1 = bf16[256,16384]{1,0:T(8,128)(2,1)} fusion(bf16[256,16384]{1,0:T(8,128)(2,1)} %bitcast.130, bf16[1,256,256]{1,2,0:T(8,128)(2,1)S(1)} %collective-permute-done.2), kind=kOutput, calls=%fused_computation.11 | convolution fusion | flops 2151677952 | bytes 16908288 | tf_op jit(solution)/shard_map/dot_general | solution.py:46
  330.3 13.5 %reshape.224 = bf16[16384,256]{1,0:T(8,128)(2,1)} reshape(bf16[256,16384]{1,0:T(8,128)(2,1)} %convolution_convert_fusion.1) | data formatting | bytes 16777216 | tf_op jit(solution)/shard_map/reshape.35
  343.8 8.1 %fusion.46 = f32[1,256,256]{1,2,0:T(8,128)S(1)} fusion(f32[256,256]{1,0:T(8,128)S(1)} %fusion.38, bf16[16384,256]{1,0:T(8,128)(2,1)} %reshape.224, bf16[16384,256]{1,0:T(8,128)(2,1)} %bitcast.127, f32[]{:T(128)} %bitcast), kind=kOutput, calls=%fused_computation.47 | convolution fusion | flops 2147614720 | bytes 17301508 | tf_op jit(solution)/shard_map/rp,krq->kpq/dot_general | solution.py:52
  351.9 20.2 %all-reduce.5 = bf16[1,256,256]{1,2,0:T(8,128)(2,1)S(1)} all-reduce(f32[1,256,256]{1,2,0:T(8,128)S(1)} %fusion.46), channel_id=1, replica_groups=mesh['leaf'=8,'bond'=4] {'bond'}, use_global_device_ids=true, to_apply=%region_5.6 | all-reduce | flops 65536 | bytes 393216 | tf_op jit(solution)/shard_map/psum | solution.py:65
  372.1 0.1 dynamic-slice_convert_fusion
  372.2 0.7 copy.61
  (8 shorter events, 0.0 us)
Async XLA Ops:
  25.5 5.8 %copy-start = (bf16[1,1,64,256]{3,2,1,0:T(8,128)(2,1)S(1)}, bf16[1,1,64,256]{3,2,1,0:T(8,128)(2,1)}, u32[]{:S(2)}) copy-start(bf16[1,1,64,256]{3,2,1,0:T(8,128)(2,1)} %param.5) | copy-start | bytes 98308
  25.5 126.1 %all-to-all-start = ((bf16[64,256,256]{2,0,1:T(8,128)(2,1)}), bf16[64,256,256]{2,0,1:T(8,128)(2,1)}, u32[]{:S(2)}, u32[]{:S(2)}) async-start(bf16[64,256,256]{2,0,1:T(8,128)(2,1)} %fusion.6), calls=%async_computation | async-start | bytes 16777216 | tf_op jit(solution)/shard_map/all_to_all | solution.py:39
  128.8 49.7 %collective-permute-start = (bf16[1,256,256]{2,1,0:T(8,128)(2,1)S(1)}, bf16[1,256,256]{2,1,0:T(8,128)(2,1)S(1)}, u32[]{:S(2)}, u32[]{:S(2)}) collective-permute-start(bf16[1,256,256]{2,1,0:T(8,128)(2,1)S(1)} %bitcast.131), channel_id=1, source_target_pairs={{0,4},{4,8},{8,12},{12,16},{16,20},{20,24},{24,28},{28,0},{1,5},{5... | collective-permute-start | bytes 393224 | tf_op jit(solution)/shard_map/ppermute | solution.py:13
  242.6 14.4 %collective-permute-start.1 = (bf16[1,256,256]{1,2,0:T(8,128)(2,1)S(1)}, bf16[1,256,256]{1,2,0:T(8,128)(2,1)S(1)}, u32[]{:S(2)}, u32[]{:S(2)}) collective-permute-start(bf16[1,256,256]{1,2,0:T(8,128)(2,1)S(1)} %all-reduce.3), channel_id=1, source_target_pairs={{0,8},{4,12},{8,16},{12,20},{16,24},{20,28},{24,0},{28,4},{1,9},{5... | collective-permute-start | bytes 393224 | tf_op jit(solution)/shard_map/ppermute | solution.py:13
  307.0 14.3 %collective-permute-start.2 = (bf16[1,256,256]{1,2,0:T(8,128)(2,1)S(1)}, bf16[1,256,256]{1,2,0:T(8,128)(2,1)S(1)}, u32[]{:S(2)}, u32[]{:S(2)}) collective-permute-start(bf16[1,256,256]{1,2,0:T(8,128)(2,1)S(1)} %all-reduce.4), channel_id=1, source_target_pairs={{0,16},{4,20},{8,24},{12,28},{16,0},{20,4},{24,8},{28,12},{1,17},{... | collective-permute-start | bytes 393224 | tf_op jit(solution)/shard_map/ppermute | solution.py:13
where the time goes:
time: 378 us; the launch traced here: 373 us
  blocking collectives  158 us (42%)
  matrix products  87.2 us (23%)
  local copies, waits for them, and re-layouts  81 us (21%)
  other arithmetic  36.5 us (10%)
  starting transfers between devices  9.03 us (2%)
    all_gather x1, blocking collectives, shards(): held_ops = lax.all_gather(leaf_ops[0], 'bond', axis=1, tiled=True)  97.5 us
    psum x3, blocking collectives, shards(): held_ops = lax.psum(partial_sum, 'bond').astype(jnp.bfloat16)  60.9 us
    another operation x3, local copies, waits for them, and re-layouts  40.6 us
    select_n x2, other arithmetic, shards(): masked = jnp.where(keep_mask, weight, jnp.zeros((), weight.dtype))  36.2 us
    dot_general x3, matrix products, shards(): jnp.einsum('acp,kacq->kpq', masked, right_mixed, preferred_element_type=j...  35.9 us
    dot_general x3, matrix products, shards(): jnp.dot(left_ops.reshape(op_count * bond_width, bond_width), by_right.res...  26.9 us
    dot_general x3, matrix products, shards(): jnp.einsum('rp,krq->kpq', by_right.reshape(-1, bond_width), left_mixed, p...  24.4 us
    unnamed x3, local copies, waits for them, and re-layouts  15.4 us
  transfers between devices with their start and end apart: 4, of which 0 were waited for; matrix products, arithmetic and copies ran while one was open for 20% of the time, Pallas kernels for 0%

commit v1 on v0

v1 whole, which is shorter than its diff:
```python
import functools

import jax
import jax.numpy as jnp
from jax import lax
from jax.experimental import pallas as pl
from jax.experimental.pallas import tpu as pltpu
from jax.sharding import PartitionSpec as P

BLOCK = 64
QMOD = 4
LEVELS = 3
ROWS = 16
GROUP = 16
CAPACITIES = (4, 6, 8, 10, 12, 16)
F32 = jnp.float32
BF16 = jnp.bfloat16
MIB = 2**20
ANY = pl.BlockSpec(memory_space=pl.ANY)
VMEM = pl.BlockSpec(memory_space=pltpu.VMEM)
SMEM = pl.BlockSpec(memory_space=pltpu.SMEM)


def dot(a, b, ca, cb):
    return lax.dot_general(a, b, (((ca,), (cb,)), ((), ())), preferred_element_type=F32)


def passed_along(array, axis, by):
    devices = lax.axis_size(axis)
    return lax.ppermute(array, axis, [(i, (i + by) % devices) for i in range(devices)])


def swapped(array, mask):
    devices = lax.axis_size("bond")
    return lax.ppermute(array, "bond", [(i, i ^ mask) for i in range(devices)])


def lookup(index_vector, charge_table, blocks):
    hits = index_vector[:, None] == blocks[None, :]
    return jnp.sum(jnp.where(hits, charge_table[None, :], 0), axis=1)


def shards_plain(isometries, leaf_ops, charges, assign):
    bond_rank = lax.axis_index("bond")
    weight = isometries[0]
    slab_rows = weight.shape[0]
    bond_width = weight.shape[1]
    op_count = leaf_ops.shape[1]
    charge_row = charges[0]
    blocks = jnp.arange(charge_row.shape[1], dtype=jnp.int32)
    left_index = (bond_rank * slab_rows + jnp.arange(slab_rows, dtype=jnp.int32)) // BLOCK
    full_index = jnp.arange(bond_width, dtype=jnp.int32) // BLOCK
    charge_left = lookup(left_index, charge_row[0], blocks)
    charge_right = lookup(full_index, charge_row[1], blocks)
    charge_parent = lookup(full_index, charge_row[2], blocks)
    charge_sum = (
        charge_left[:, None, None] + charge_right[None, :, None] - charge_parent[None, None, :]
    )
    keep_mask = jnp.mod(charge_sum, QMOD) == 0
    masked = jnp.where(keep_mask, weight, jnp.zeros((), weight.dtype))
    by_right = lax.all_to_all(masked, "bond", split_axis=1, concat_axis=0, tiled=True)
    take_left = (assign[0] != 1).astype(F32)
    take_right = (assign[0] != 0).astype(F32)
    held_ops = lax.all_gather(leaf_ops[0], "bond", axis=1, tiled=True)
    for level_now in range(1, LEVELS + 1):
        reach_by = 2 ** (level_now - 1)
        left_ops = passed_along(held_ops, "leaf", reach_by)
        left_mixed = jnp.dot(
            left_ops.reshape(op_count * bond_width, bond_width),
            by_right.reshape(bond_width, -1),
            preferred_element_type=F32,
        ).astype(BF16)
        left_mixed = left_mixed.reshape(op_count, -1, bond_width)
        left_part = jnp.einsum(
            "rp,krq->kpq",
            by_right.reshape(-1, bond_width),
            left_mixed,
            preferred_element_type=F32,
        )
        right_mixed = jnp.einsum(
            "kcb,abq->kacq", held_ops, masked, preferred_element_type=F32
        ).astype(BF16)
        right_part = jnp.einsum("acp,kacq->kpq", masked, right_mixed, preferred_element_type=F32)
        partial_sum = take_left[:, None, None] * left_part + take_right[:, None, None] * right_part
        held_ops = lax.psum(partial_sum, "bond").astype(BF16)
    result = lax.dynamic_slice_in_dim(held_ops, bond_rank * slab_rows, slab_rows, 1)
    return result[None]


CHARGES_AT = 2


def fits(info, blocks, left, right, parent):
    total = (
        info[CHARGES_AT + left]
        + info[CHARGES_AT + blocks + right]
        - info[CHARGES_AT + 2 * blocks + parent]
    )
    return lax.rem(total + QMOD, QMOD) == 0


def pieces_before(info, blocks, left, right, parent):
    count = jnp.int32(0)
    for k in range(blocks):
        for p in range(blocks):
            ahead = (k * blocks + p) < (right * blocks + parent)
            count += (fits(info, blocks, left, k, p) & ahead).astype(jnp.int32)
    return count


def pieces_of(info, blocks, left):
    return pieces_before(info, blocks, left, blocks, 0)


def add_group(op, mats, total):
    count, width = mats.shape[0], mats.shape[1]
    mixed = [dot(op, mats[j], 1, 0).astype(BF16) for j in range(count)]
    return total + dot(
        mats.reshape(count * width, width), jnp.concatenate(mixed, 0), 0, 0
    )


def halves_swapped(x):
    return jnp.concatenate([x[..., BLOCK:], x[..., :BLOCK]], axis=-1)


def pack_kernel(blocks, partners, info, weight, branch, *rest):
    groups = len(CAPACITIES)
    outs = rest[: partners * groups]
    stage, turn, sems = rest[partners * groups :]
    m, k = pl.program_id(0), pl.program_id(1)
    rank = info[0]
    area = GROUP * ROWS
    slab = weight.shape[0]
    width = weight.shape[-1]

    @pl.when((m == 0) & (k == 0))
    def _():
        to = lax.broadcasted_iota(jnp.int32, (area, area), 0)
        at = lax.broadcasted_iota(jnp.int32, (area, area), 1)
        turn[...] = jnp.where(at == (to % GROUP) * ROWS + to // GROUP, 1.0, 0.0).astype(BF16)
        need = lax.fori_loop(
            0, blocks, lambda d, most: jnp.maximum(most, pieces_of(info, blocks, d)), jnp.int32(0)
        )
        step = jnp.int32(1)
        for cap in CAPACITIES[:-1]:
            step += (need > cap).astype(jnp.int32)
        branch[0] = jnp.where(info[1] == 1, 0, step)

    allowed = [fits(info, blocks, rank, k, p) for p in range(blocks)]
    some = functools.reduce(jnp.logical_or, allowed)

    @pl.when(some & (info[1] != 1))
    def _():
        turned = []
        for g in range(slab // GROUP):
            rows = weight[g * GROUP : (g + 1) * GROUP].reshape(area, width)
            turned.append(dot(turn[...], rows, 1, 0).astype(BF16))
        half = len(turned) // 2
        slot = pieces_before(info, blocks, rank, k, 0)
        for p in range(blocks):

            @pl.when(allowed[p])
            def _():
                for h in range(half):
                    low = turned[h][:, p * BLOCK : (p + 1) * BLOCK]
                    high = turned[h + half][:, p * BLOCK : (p + 1) * BLOCK]
                    both = jnp.concatenate([low, high], axis=1).reshape(ROWS, GROUP, 2 * BLOCK)
                    stage[m, k * blocks + p, :, h * GROUP : (h + 1) * GROUP, :] = both
                first = 0
                for g, cap in enumerate(CAPACITIES):
                    for n in range(partners):

                        @pl.when((slot >= first) & (slot < cap) & (m == n))
                        def _():
                            pltpu.make_async_copy(
                                stage.at[n, k * blocks + p],
                                outs[n * groups + g].at[slot - first],
                                sems.at[n, k * blocks + p],
                            ).start()

                    first = cap

            slot = slot + allowed[p].astype(jnp.int32)

    @pl.when((m == partners - 1) & (k == blocks - 1) & (info[1] != 1))
    def _():
        @pl.loop(0, blocks * blocks)
        def _(f):
            @pl.when(fits(info, blocks, rank, f // blocks, f % blocks))
            def _():
                for n in range(partners):
                    pltpu.make_async_copy(
                        stage.at[n, f], outs[n * groups].at[0], sems.at[n, f]
                    ).wait()


def pack(info, weight):
    slab, width = weight.shape[0], weight.shape[1]
    partners = lax.axis_size("bond")
    blocks = width // BLOCK
    cut = weight.reshape(slab, blocks, partners, ROWS, width)
    sizes = [b - a for a, b in zip((0,) + CAPACITIES[:-1], CAPACITIES)]
    piece = (ROWS, slab // 2, 2 * BLOCK)
    branch, *packed = pl.pallas_call(
        functools.partial(pack_kernel, blocks, partners),
        grid_spec=pltpu.PrefetchScalarGridSpec(
            num_scalar_prefetch=1,
            grid=(partners, blocks),
            in_specs=[
                pl.BlockSpec(
                    (slab, None, None, ROWS, width), lambda m, k, info: (0, k, info[0] ^ m, 0, 0)
                )
            ],
            out_specs=[SMEM] + [ANY] * (partners * len(sizes)),
            scratch_shapes=[
                pltpu.VMEM((partners, blocks * blocks) + piece, BF16),
                pltpu.VMEM((GROUP * ROWS, GROUP * ROWS), BF16),
                pltpu.SemaphoreType.DMA((partners, blocks * blocks)),
            ],
        ),
        out_shape=[jax.ShapeDtypeStruct((1,), jnp.int32)]
        + [jax.ShapeDtypeStruct((n,) + piece, BF16) for n in sizes] * partners,
        compiler_params=pltpu.CompilerParams(vmem_limit_bytes=24 * MIB),
        name="pack",
    )(info, cut)
    groups = len(sizes)
    return branch[0], [packed[m * groups : (m + 1) * groups] for m in range(partners)]


def first_left_kernel(partners, info, op, before, *rest):
    groups = len(CAPACITIES)
    parts = rest[: partners * groups]
    mats, after, held, sems = rest[partners * groups :]
    rank = info[0]
    width = op.shape[0]
    blocks = width // BLOCK
    slab = 2 * held.shape[3]
    starts = (0,) + CAPACITIES[:-1]

    def load(m, g):
        return pltpu.make_async_copy(
            parts[m * groups + g],
            held.at[m, pl.ds(starts[g], CAPACITIES[g] - starts[g])],
            sems.at[m, g],
        )

    after[...] = before[...]

    @pl.when(info[1] != 1)
    def _():
        counts = [pieces_of(info, blocks, rank ^ m) for m in range(partners)]
        for m in range(partners):
            for g in range(groups):
                pl.when(counts[m] > starts[g])(load(m, g).start)

        @pl.loop(0, mats.shape[0])
        def _(j):
            mats[j] = jnp.zeros((width, width), BF16)

        for m in range(partners):
            for g in range(groups):
                pl.when(counts[m] > starts[g])(load(m, g).wait)

        @pl.loop(0, partners * blocks)
        def _(n):
            m, k = n // blocks, n % blocks
            source = rank ^ m
            slot = pieces_before(info, blocks, source, k, 0)
            for p in range(blocks):
                allowed = fits(info, blocks, source, k, p)

                @pl.when(allowed)
                def _():
                    piece = held[m, slot]
                    other = halves_swapped(piece)
                    tile = p // 2 * 2 * BLOCK
                    lane = lax.broadcasted_iota(jnp.int32, piece.shape, 2)
                    keep = lane < BLOCK if p % 2 == 0 else lane >= BLOCK
                    parts = (piece, other) if p % 2 == 0 else (other, piece)
                    for i, part in enumerate(parts):
                        at = pl.multiple_of(source * slab + i * (slab // 2), slab // 2)
                        where = (
                            pl.ds(pl.multiple_of(k * ROWS, ROWS), ROWS),
                            pl.ds(at, slab // 2),
                            slice(tile, tile + 2 * BLOCK),
                        )
                        mats[where] = jnp.where(keep, part, mats[where])

                slot = slot + allowed.astype(jnp.int32)

        @pl.loop(0, mats.shape[0] // GROUP)
        def _(c):
            group = mats[pl.ds(pl.multiple_of(c * GROUP, GROUP), GROUP)]
            after[...] = add_group(op[...], group, after[...])


def first_left(info, op, before, parts):
    partners, groups = len(parts), len(parts[0])
    width = op.shape[0]
    piece = parts[0][0].shape[1:]
    flat = [group for part in parts for group in part]
    return pl.pallas_call(
        functools.partial(first_left_kernel, partners),
        in_specs=[SMEM, VMEM, VMEM] + [ANY] * len(flat),
        out_specs=[VMEM, VMEM],
        out_shape=[
            jax.ShapeDtypeStruct((ROWS * (width // BLOCK), width, width), BF16),
            jax.ShapeDtypeStruct((width, width), F32),
        ],
        scratch_shapes=[
            pltpu.VMEM((partners, CAPACITIES[-1]) + piece, BF16),
            pltpu.SemaphoreType.DMA((partners, groups)),
        ],
        compiler_params=pltpu.CompilerParams(vmem_limit_bytes=32 * MIB),
        name="first_left",
    )(info, op, before, *flat)


def mask_of(info, width):
    blocks = width // BLOCK

    def spread(shape, axis, at):
        block = lax.broadcasted_iota(jnp.int32, shape, axis) // BLOCK
        charge = jnp.zeros(shape, jnp.int32)
        for k in range(blocks):
            charge = jnp.where(block == k, info[at + k], charge)
        return charge

    right = spread((width, width), 0, CHARGES_AT + blocks)
    parent = spread((width, width), 1, CHARGES_AT + 2 * blocks)
    left = info[CHARGES_AT + info[0]]
    return jnp.where(lax.rem(left + right - parent + QMOD, QMOD) == 0, 1.0, 0.0).astype(BF16)


def side_kernel(not_if, masked, per, info, op, before, mats, after, *scratch):
    after[...] = before[...]

    @pl.when(info[1] != not_if)
    def _():
        mask = mask_of(info, op.shape[0]) if masked else None
        if scratch:
            held, sems = scratch

            def load(c):
                return pltpu.make_async_copy(mats.at[pl.ds(c * per, per)], held.at[c], sems.at[c])

            @pl.loop(0, held.shape[0])
            def _(c):
                load(c).start()

        @pl.loop(0, mats.shape[0] // per)
        def _(c):
            if scratch:
                load(c).wait()
                group = held[c]
            else:
                group = mats[pl.ds(pl.multiple_of(c * per, per), per)]
            if masked:
                group = group * mask[None]
            after[...] = add_group(op[...], group, after[...])


def side(not_if, info, op, before, mats, masked, per, streamed):
    width = op.shape[0]
    total = mats.shape[0]
    return pl.pallas_call(
        functools.partial(side_kernel, not_if, masked, per),
        in_specs=[SMEM, VMEM, VMEM, ANY if streamed else VMEM],
        out_specs=VMEM,
        out_shape=jax.ShapeDtypeStruct((width, width), F32),
        scratch_shapes=[
            pltpu.VMEM((total // per, per, width, width), BF16),
            pltpu.SemaphoreType.DMA((total // per,)),
        ]
        if streamed
        else [],
        compiler_params=pltpu.CompilerParams(vmem_limit_bytes=(24 if streamed else 12) * MIB),
        cost_estimate=pl.CostEstimate(
            flops=4 * total * width**3, bytes_accessed=2 * total * width**2, transcendentals=0
        ),
        name="side",
    )(info, op, before, mats)


def shards(isometries, leaf_ops, charges, assign):
    rank = lax.axis_index("bond")
    partners = lax.axis_size("bond")
    weight = isometries[0]
    slab, width = weight.shape[0], weight.shape[1]
    own = leaf_ops[0, 0]
    left = passed_along(own, "leaf", 1)
    info = jnp.concatenate([rank.reshape(1).astype(jnp.int32), assign[0], charges[0].reshape(-1)])
    zeros = jnp.zeros((width, width), F32)

    def gathered(part):
        both = jnp.stack([part] + [swapped(part, m) for m in range(1, partners)])
        return jnp.take(both, jnp.arange(partners) ^ rank, axis=0)

    def ops_of(own, left):
        full = gathered(jnp.stack([own, left]))
        return full[:, 0].reshape(width, width), full[:, 1].reshape(width, width)

    branch, packed = pack(info, weight)

    def exchange(groups, info, weight, own, left, packed):
        op, left_op = ops_of(own, left)
        come = [
            [swapped(packed[m][g], m) for g in range(groups)]
            + [jnp.zeros_like(part) for part in packed[m][groups:]]
            for m in range(1, partners)
        ]
        total = side(0, info, op, zeros, weight, True, 8, True)
        return total, left_op, come

    total, left_op, come = lax.switch(
        branch,
        [functools.partial(exchange, g) for g in range(len(CAPACITIES) + 1)],
        info, weight, own, left, packed,
    )
    mats, total = first_left(info, left_op, total, [packed[0]] + come)
    for level in range(2, LEVELS + 1):
        sent = total.astype(BF16)
        come = [swapped(sent, m) for m in range(1, partners)]
        op = (total + sum(c.astype(F32) for c in come)).astype(BF16)
        left_op = passed_along(op, "leaf", 2 ** (level - 1))
        total = side(0, info, op, zeros, weight, True, 32, False)
        total = side(1, info, left_op, total, mats, False, 32, False)

    def rows_of(m):
        return lax.dynamic_slice_in_dim(total, (rank ^ m) * slab, slab, 0)

    result = rows_of(0)
    for m in range(1, partners):
        result = result + swapped(rows_of(m), m)
    return result.astype(BF16)[None, None]


def solution(mesh):
    in_specs = (
        P("leaf", "bond", None, None),
        P("leaf", None, "bond", None),
        P("leaf", None, None),
        P("leaf", None),
    )
    out_specs = P("leaf", None, "bond", None)
    partners = mesh.shape["bond"]

    def whole(isometries, leaf_ops, charges, assign):
        width = isometries.shape[1]
        fits = (
            partners & (partners - 1) == 0
            and width // partners == BLOCK
            and BLOCK == partners * ROWS
            and charges.shape[2] * BLOCK == width
            and leaf_ops.shape[1] == 1
        )
        return jax.shard_map(
            shards if fits else shards_plain,
            mesh=mesh, in_specs=in_specs, out_specs=out_specs, check_vma=False,
        )(isometries, leaf_ops, charges, assign)

    return whole
```

time: 378 us -> 145 us (0.38)
  blocking collectives: 158 us -> 0 us
  matrix products: 87.2 us -> 0 us
  local copies, waits for them, and re-layouts: 81 us -> 13.4 us
  waiting for transfers between devices: 0.01 us -> 56.3 us
  Pallas kernels: 0 us -> 44 us
  other arithmetic: 36.5 us -> 1.72 us
  starting transfers between devices: 9.03 us -> 26.2 us
    all_gather x1 -> x0, blocking collectives: 97.5 us -> none  [shards(): held_ops = lax.all_gather(leaf_ops[0], 'bond', axis=1, tiled=True)]
    dot_general x9 -> x0, matrix products: 87.2 us -> none  [the longest x3 35.9 us: shards(): jnp.einsum('acp,kacq->kpq', masked, right_mixed, preferred_element_type=j...]
    psum x3 -> x0, blocking collectives: 60.9 us -> none  [shards(): held_ops = lax.psum(partial_sum, 'bond').astype(jnp.bfloat16)]
    ppermute x0 -> x18, waiting for transfers between devices: none -> 47.2 us  [swapped(): return lax.ppermute(array, 'bond', [(i, i ^ mask) for i in range(devices)])]
    pallas_call x0 -> x7, Pallas kernels: none -> 44 us  [the longest x5 16.1 us: side(): pl.pallas_call(functools.partial(side_kernel, not_if, masked, per), in_sp...]
    select_n x4 -> x2, other arithmetic: 36.2 us -> 0.1 us  [gathered(): return jnp.take(both, jnp.arange(partners) ^ rank, axis=0)]
    another operation x3 -> x13, local copies, waits for them, and re-layouts: 40.6 us -> 9.4 us  [the longest x12 9.32 us: whole(): jax.shard_map(shards if fits else shards_plain, mesh=mesh, in_specs=in_sp...]
    ppermute x0 -> x18, starting transfers between devices: none -> 25.7 us  [swapped(): return lax.ppermute(array, 'bond', [(i, i ^ mask) for i in range(devices)])]
  transfers between devices with their start and end apart: 4 -> 21, of which waited for: 0 -> 13; matrix products, arithmetic and copies ran while one was open for 20% -> 1% of each run, Pallas kernels for 0% -> 14%
where the time goes in v1:
time: 145 us; the launch traced here: 143 us
  waiting for transfers between devices  56.3 us (39%)
  Pallas kernels  44 us (30%)
  starting transfers between devices  26.2 us (18%)
  local copies, waits for them, and re-layouts  13.4 us (9%)
  other arithmetic  1.72 us (1%)
  between operations  1.45 us (1%)
    ppermute x18, waiting for transfers between devices, swapped(): return lax.ppermute(array, 'bond', [(i, i ^ mask) for i in range(devices)])  47.2 us
    ppermute x18, starting transfers between devices, swapped(): return lax.ppermute(array, 'bond', [(i, i ^ mask) for i in range(devices)])  25.7 us
    pallas_call x5, Pallas kernels, side(): pl.pallas_call(functools.partial(side_kernel, not_if, masked, per), in_sp...  16.1 us
    pallas_call x1, Pallas kernels, pack(): pl.pallas_call(functools.partial(pack_kernel, blocks, partners), grid_spe...  15.9 us
    pallas_call x1, Pallas kernels, first_left(): pl.pallas_call(functools.partial(first_left_kernel, partners), in_specs=[...  12 us
    another operation x12, local copies, waits for them, and re-layouts, whole(): jax.shard_map(shards if fits else shards_plain, mesh=mesh, in_specs=in_sp...  9.32 us
    ppermute x3, waiting for transfers between devices, passed_along(): lax.ppermute(array, axis, [(i, (i + by) % devices) for i in range(devices)])  9.08 us
    unnamed x8, local copies, waits for them, and re-layouts  3.39 us
  transfers between devices with their start and end apart: 21, of which 13 were waited for; matrix products, arithmetic and copies ran while one was open for 1% of the time, Pallas kernels for 14%

profile of v1, /device:TPU:0, one launch (start us, length us, event | category | flops | bytes accessed | tf_op | source)
XLA Modules:
  0.0 143.2 jit_solution(18260942626480671654)
XLA Ops:
  2.0 15.9 %pack.1 = (s32[1]{0:T(128)}, bf16[4,16,32,128]{3,2,1,0:T(8,128)(2,1)S(1)}, bf16[2,16,32,128]{3,2,1,0:T(8,128)(2,1)S(1)}, bf16[2,16,32,128]{3,2,1,0:T(8,128)(2,1)...) custom-call(s32[14]{0:T(128)S(1)} %pad_add_fusion.info, ...), custom_call_target="tpu_custom_call" | custom-call | tf_op jit(solution)/shard_map/pack/pallas_call | solution.py:205
  18.6 57.7 %conditional.1 = (f32[256,256]{1,0:T(8,128)S(1)}, bf16[256,256]{1,0:T(8,128)(2,1)S(1)}, bf16[4,16,32,128]{3,2,1,0:T(8,128)(2,1)}, bf16[2,16,32,128]{3,2,1,0:T(8,...) conditional(s32[]{:T(128)} %bitcast.59, ...), branch_computations={%region_0.2_spmd, %region_1.3_spmd, %region_2.4_spmd, %region_3.5_... | conditional | flops 4295525376 | bytes 36901932 | solution.py:416
  18.7 2.6 %collective-permute-start.9 = (bf16[2,64,256]{2,1,0:T(8,128)(2,1)S(1)}, bf16[2,64,256]{2,1,0:T(8,128)(2,1)S(1)}, u32[]{:S(2)}, u32[]{:S(2)}) collective-permute-start(bf16[2,64,256]{2,1,0:T(8,128)(2,1)S(1)} %get-tuple-element.405), channel_id=1, source_target_pairs={{0,1},{1,0},{2,3},{3,2},{4,5},{5,4},{6,7},{7,6},{8,9},{9,8},{10,11... | collective-permute-start | bytes 196616 | tf_op jit(solution)/shard_map/cond/branch_2_fun/ppermute | solution.py:35
  21.2 3.6 %collective-permute-start.10 = (bf16[2,64,256]{2,1,0:T(8,128)(2,1)S(1)}, bf16[2,64,256]{2,1,0:T(8,128)(2,1)S(1)}, u32[]{:S(2)}, u32[]{:S(2)}) collective-permute-start(bf16[2,64,256]{2,1,0:T(8,128)(2,1)S(1)} %get-tuple-element.405), channel_id=1, source_target_pairs={{0,2},{1,3},{2,0},{3,1},{4,6},{5,7},{6,4},{7,5},{8,10},{9,11},{10,... | collective-permute-start | bytes 196616 | tf_op jit(solution)/shard_map/cond/branch_2_fun/ppermute | solution.py:35
  24.8 1.5 %collective-permute-start.12 = (bf16[4,16,32,128]{3,2,1,0:T(8,128)(2,1)S(1)}, bf16[4,16,32,128]{3,2,1,0:T(8,128)(2,1)}, u32[]{:S(2)}, u32[]{:S(2)}) collective-permute-start(bf16[4,16,32,128]{3,2,1,0:T(8,128)(2,1)S(1)} %get-tuple-element.220), channel_id=1, source_target_pairs={{0,1},{1,0},{2,3},{3,2},{4,5},{5,4},{6,7},{7,6},{8,9},{9,8},{10,11... | collective-permute-start | bytes 1572872 | tf_op jit(solution)/shard_map/cond/branch_2_fun/ppermute | solution.py:35
  26.3 2.0 %collective-permute-start.14 = (bf16[4,16,32,128]{3,2,1,0:T(8,128)(2,1)}, bf16[4,16,32,128]{3,2,1,0:T(8,128)(2,1)}, u32[]{:S(2)}, u32[]{:S(2)}) collective-permute-start(bf16[4,16,32,128]{3,2,1,0:T(8,128)(2,1)} %get-tuple-element.222), channel_id=1, source_target_pairs={{0,2},{1,3},{2,0},{3,1},{4,6},{5,7},{6,4},{7,5},{8,10},{9,11},{10,... | collective-permute-start | bytes 1572872 | tf_op jit(solution)/shard_map/cond/branch_2_fun/ppermute | solution.py:35
  28.5 1.3 collective-permute-start.13
  30.6 1.3 collective-permute-start.15
  32.6 24.2 %collective-permute-done.13 = bf16[2,16,32,128]{3,2,1,0:T(8,128)(2,1)} collective-permute-done((bf16[2,16,32,128]{3,2,1,0:T(8,128)(2,1)S(1)}, bf16[2,16,32,128]{3,2,1,0:T(8,128)(2,1)}, u32[]{:S(2)}, u32[]{:S(2)}) %collective-permute-start.13) | collective-permute-done | bytes 262176 | tf_op jit(solution)/shard_map/cond/branch_2_fun/ppermute | solution.py:35
  56.9 2.5 %collective-permute-start.17 = (bf16[2,16,32,128]{3,2,1,0:T(8,128)(2,1)}, bf16[2,16,32,128]{3,2,1,0:T(8,128)(2,1)}, u32[]{:S(2)}, u32[]{:S(2)}) collective-permute-start(bf16[2,16,32,128]{3,2,1,0:T(8,128)(2,1)} %get-tuple-element.225), channel_id=1, source_target_pairs={{0,3},{1,2},{2,1},{3,0},{4,7},{5,6},{6,5},{7,4},{8,11},{9,10},{10,... | collective-permute-start | bytes 786440 | tf_op jit(solution)/shard_map/cond/branch_2_fun/ppermute | solution.py:35
  60.0 6.9 %collective-permute-done.17 = bf16[2,16,32,128]{3,2,1,0:T(8,128)(2,1)} collective-permute-done((bf16[2,16,32,128]{3,2,1,0:T(8,128)(2,1)}, bf16[2,16,32,128]{3,2,1,0:T(8,128)(2,1)}, u32[]{:S(2)}, u32[]{:S(2)}) %collective-permute-start.17) | collective-permute-done | bytes 262176 | tf_op jit(solution)/shard_map/cond/branch_2_fun/ppermute | solution.py:35
  67.0 0.9 broadcast.40
  76.3 12.0 %first_left.1 = (bf16[64,256,256]{2,1,0:T(8,128)(2,1)S(1)}, f32[256,256]{1,0:T(8,128)S(1)}) custom-call(s32[14]{0:T(128)S(1)} %pad_add_fusion.info, bf16[256,256]{1,0:T(8,128)(2,1)S(1)} %get-tuple-element.366.op, f32[256,256]{1,0:T(8,128)S(1)} %get-tuple-element.367.before, bf16[4,16,32,128]{3,2,1,0:T(8,128)(2,1)S(1)} %get-tuple-element.368.rest_0_, ...), custom_call_target="tpu_custom_call" | custom-call | tf_op jit(solution)/shard_map/first_left/pallas_call | solution.py:303
  88.4 0.9 collective-permute-start.85
  89.3 1.4 collective-permute-start.86
  90.7 1.3 collective-permute-start.87
  91.9 1.5 %collective-permute-done.85 = bf16[256,256]{1,0:T(8,128)(2,1)S(1)} collective-permute-done((bf16[256,256]{1,0:T(8,128)(2,1)S(1)}, bf16[256,256]{1,0:T(8,128)(2,1)S(1)}, u32[]{:S(2)}, u32[]{:S(2)}) %collective-permute-start.85) | collective-permute-done | bytes 131104 | tf_op jit(solution)/shard_map/ppermute | solution.py:35
  94.3 4.9 %collective-permute-done.87 = bf16[256,256]{1,0:T(8,128)(2,1)S(1)} collective-permute-done((bf16[256,256]{1,0:T(8,128)(2,1)S(1)}, bf16[256,256]{1,0:T(8,128)(2,1)S(1)}, u32[]{:S(2)}, u32[]{:S(2)}) %collective-permute-start.87) | collective-permute-done | bytes 131104 | tf_op jit(solution)/shard_map/ppermute | solution.py:35
  99.8 6.6 %collective-permute-done.88.op = bf16[256,256]{1,0:T(8,128)(2,1)S(1)} collective-permute-done((bf16[256,256]{1,0:T(8,128)(2,1)S(1)}, bf16[256,256]{1,0:T(8,128)(2,1)S(1)}, u32[]{:S(2)}, u32[]{:S(2)}) %collective-permute-start.88) | collective-permute-done | bytes 131104 | tf_op jit(solution)/shard_map/ppermute | solution.py:30
  106.5 5.6 %side.19 = f32[256,256]{1,0:T(8,128)S(1)} custom-call(s32[14]{0:T(128)S(1)} %pad_add_fusion.info, bf16[256,256]{1,0:T(8,128)(2,1)S(1)} %collective-permute-done.88.op, f32[256,256]{1,0:T(8,128)S(1)} %side.18.before, bf16[64,256,256]{2,1,0:T(8,128)(2,1)S(1)} %get-tuple-element.393.mats), custom_call_target="tpu_custom_call" | custom-call | flops 4294967296 | bytes 8388608 | tf_op jit(solution)/shard_map/side/pallas_call | solution.py:367
  112.5 1.8 %collective-permute-start.90 = (bf16[256,256]{1,0:T(8,128)(2,1)S(1)}, bf16[256,256]{1,0:T(8,128)(2,1)S(1)}, u32[]{:S(2)}, u32[]{:S(2)}) collective-permute-start(bf16[256,256]{1,0:T(8,128)(2,1)S(1)} %convert_element_type.38), channel_id=1, source_target_pairs={{0,2},{1,3},{2,0},{3,1},{4,6},{5,7},{6,4},{7,5},{8,10},{9,11},{10,... | collective-permute-start | bytes 393224 | tf_op jit(solution)/shard_map/ppermute | solution.py:35
  114.2 1.4 collective-permute-start.91
  115.7 2.5 %collective-permute-done.89 = bf16[256,256]{1,0:T(8,128)(2,1)S(1)} collective-permute-done((bf16[256,256]{1,0:T(8,128)(2,1)S(1)}, bf16[256,256]{1,0:T(8,128)(2,1)S(1)}, u32[]{:S(2)}, u32[]{:S(2)}) %collective-permute-start.89) | collective-permute-done | bytes 131104 | tf_op jit(solution)/shard_map/ppermute | solution.py:35
  118.2 2.1 %collective-permute-done.90 = bf16[256,256]{1,0:T(8,128)(2,1)S(1)} collective-permute-done((bf16[256,256]{1,0:T(8,128)(2,1)S(1)}, bf16[256,256]{1,0:T(8,128)(2,1)S(1)}, u32[]{:S(2)}, u32[]{:S(2)}) %collective-permute-start.90) | collective-permute-done | bytes 131104 | tf_op jit(solution)/shard_map/ppermute | solution.py:35
  120.4 3.4 %side.20.before = f32[256,256]{1,0:T(8,128)S(1)} custom-call(s32[14]{0:T(128)S(1)} %pad_add_fusion.info, bf16[256,256]{1,0:T(8,128)(2,1)S(1)} %add_convert_fusion.op, f32[256,256]{1,0:T(8,128)S(1)} %broadcast_in_dim.36.before, bf16[64,256,256]{2,1,0:T(8,128)(2,1)} %bitcast.87), custom_call_target="tpu_custom_call" | custom-call | flops 4294967296 | bytes 8388608 | tf_op jit(solution)/shard_map/side/pallas_call | solution.py:367
  123.8 2.4 %collective-permute-done.92.op = bf16[256,256]{1,0:T(8,128)(2,1)S(1)} collective-permute-done((bf16[256,256]{1,0:T(8,128)(2,1)S(1)}, bf16[256,256]{1,0:T(8,128)(2,1)S(1)}, u32[]{:S(2)}, u32[]{:S(2)}) %collective-permute-start.92) | collective-permute-done | bytes 131104 | tf_op jit(solution)/shard_map/ppermute | solution.py:30
  126.3 3.4 %copy-done.1 = bf16[64,256,256]{2,1,0:T(8,128)(2,1)S(1)} copy-done((bf16[64,256,256]{2,1,0:T(8,128)(2,1)S(1)}, bf16[64,256,256]{2,1,0:T(8,128)(2,1)}, u32[]{:S(2)}) %copy-start.1) | copy-done | bytes 8388632
  129.6 5.9 %side.21 = f32[256,256]{1,0:T(8,128)S(1)} custom-call(s32[14]{0:T(128)S(1)} %pad_add_fusion.info, bf16[256,256]{1,0:T(8,128)(2,1)S(1)} %collective-permute-done.92.op, f32[256,256]{1,0:T(8,128)S(1)} %side.20.before, bf16[64,256,256]{2,1,0:T(8,128)(2,1)S(1)} %copy-done.1), custom_call_target="tpu_custom_call" | custom-call | flops 4294967296 | bytes 8388608 | tf_op jit(solution)/shard_map/side/pallas_call | solution.py:367
  135.5 1.2 collective-permute-start.93
  137.4 1.7 %collective-permute-start.95 = (f32[64,256]{1,0:T(8,128)S(1)}, f32[64,256]{1,0:T(8,128)S(1)}, u32[]{:S(2)}, u32[]{:S(2)}) collective-permute-start(f32[64,256]{1,0:T(8,128)S(1)} %get-tuple-element.423), channel_id=1, source_target_pairs={{0,3},{1,2},{2,1},{3,0},{4,7},{5,6},{6,5},{7,4},{8,11},{9,10},{10,... | collective-permute-start | bytes 196616 | tf_op jit(solution)/shard_map/ppermute | solution.py:35
  139.9 1.0 collective-permute-done.94
  141.0 1.6 %collective-permute-done.95 = f32[64,256]{1,0:T(8,128)S(1)} collective-permute-done((f32[64,256]{1,0:T(8,128)S(1)}, f32[64,256]{1,0:T(8,128)S(1)}, u32[]{:S(2)}, u32[]{:S(2)}) %collective-permute-start.95) | collective-permute-done | bytes 65568 | tf_op jit(solution)/shard_map/ppermute | solution.py:35
  (57 shorter events, 16.4 us)
Async XLA Ops:
  0.0 18.6 %copy-start.3 = (bf16[1,1,64,256]{3,2,1,0:T(8,128)(2,1)S(1)}, bf16[1,1,64,256]{3,2,1,0:T(8,128)(2,1)}, u32[]{:S(2)}) copy-start(bf16[1,1,64,256]{3,2,1,0:T(8,128)(2,1)} %param.14) | copy-start | bytes 98308
  0.0 18.6 %collective-permute-start.84 = (bf16[64,256]{1,0:T(8,128)(2,1)}, bf16[64,256]{1,0:T(8,128)(2,1)S(1)}, u32[]{:S(2)}, u32[]{:S(2)}) collective-permute-start(bf16[64,256]{1,0:T(8,128)(2,1)} %bitcast.89), channel_id=1, source_target_pairs={{0,4},{4,8},{8,12},{12,16},{16,20},{20,24},{24,28},{28,0},{1,5},{5... | collective-permute-start | bytes 98312 | tf_op jit(solution)/shard_map/ppermute | solution.py:30
  18.7 9.7 %collective-permute-start.9 = (bf16[2,64,256]{2,1,0:T(8,128)(2,1)S(1)}, bf16[2,64,256]{2,1,0:T(8,128)(2,1)S(1)}, u32[]{:S(2)}, u32[]{:S(2)}) collective-permute-start(bf16[2,64,256]{2,1,0:T(8,128)(2,1)S(1)} %get-tuple-element.405), channel_id=1, source_target_pairs={{0,1},{1,0},{2,3},{3,2},{4,5},{5,4},{6,7},{7,6},{8,9},{9,8},{10,11... | collective-permute-start | bytes 196616 | tf_op jit(solution)/shard_map/cond/branch_2_fun/ppermute | solution.py:35
  21.2 7.3 %collective-permute-start.10 = (bf16[2,64,256]{2,1,0:T(8,128)(2,1)S(1)}, bf16[2,64,256]{2,1,0:T(8,128)(2,1)S(1)}, u32[]{:S(2)}, u32[]{:S(2)}) collective-permute-start(bf16[2,64,256]{2,1,0:T(8,128)(2,1)S(1)} %get-tuple-element.405), channel_id=1, source_target_pairs={{0,2},{1,3},{2,0},{3,1},{4,6},{5,7},{6,4},{7,5},{8,10},{9,11},{10,... | collective-permute-start | bytes 196616 | tf_op jit(solution)/shard_map/cond/branch_2_fun/ppermute | solution.py:35
  24.8 5.8 %collective-permute-start.11 = (bf16[2,64,256]{2,1,0:T(8,128)(2,1)S(1)}, bf16[2,64,256]{2,1,0:T(8,128)(2,1)S(1)}, u32[]{:S(2)}, u32[]{:S(2)}) collective-permute-start(bf16[2,64,256]{2,1,0:T(8,128)(2,1)S(1)} %get-tuple-element.405), channel_id=1, source_target_pairs={{0,3},{1,2},{2,1},{3,0},{4,7},{5,6},{6,5},{7,4},{8,11},{9,10},{10,... | collective-permute-start | bytes 196616 | tf_op jit(solution)/shard_map/cond/branch_2_fun/ppermute | solution.py:35
  24.8 42.2 %collective-permute-start.12 = (bf16[4,16,32,128]{3,2,1,0:T(8,128)(2,1)S(1)}, bf16[4,16,32,128]{3,2,1,0:T(8,128)(2,1)}, u32[]{:S(2)}, u32[]{:S(2)}) collective-permute-start(bf16[4,16,32,128]{3,2,1,0:T(8,128)(2,1)S(1)} %get-tuple-element.220), channel_id=1, source_target_pairs={{0,1},{1,0},{2,3},{3,2},{4,5},{5,4},{6,7},{7,6},{8,9},{9,8},{10,11... | collective-permute-start | bytes 1572872 | tf_op jit(solution)/shard_map/cond/branch_2_fun/ppermute | solution.py:35
  26.3 40.7 %collective-permute-start.14 = (bf16[4,16,32,128]{3,2,1,0:T(8,128)(2,1)}, bf16[4,16,32,128]{3,2,1,0:T(8,128)(2,1)}, u32[]{:S(2)}, u32[]{:S(2)}) collective-permute-start(bf16[4,16,32,128]{3,2,1,0:T(8,128)(2,1)} %get-tuple-element.222), channel_id=1, source_target_pairs={{0,2},{1,3},{2,0},{3,1},{4,6},{5,7},{6,4},{7,5},{8,10},{9,11},{10,... | collective-permute-start | bytes 1572872 | tf_op jit(solution)/shard_map/cond/branch_2_fun/ppermute | solution.py:35
  28.3 38.7 %collective-permute-start.16 = (bf16[4,16,32,128]{3,2,1,0:T(8,128)(2,1)}, bf16[4,16,32,128]{3,2,1,0:T(8,128)(2,1)}, u32[]{:S(2)}, u32[]{:S(2)}) collective-permute-start(bf16[4,16,32,128]{3,2,1,0:T(8,128)(2,1)} %get-tuple-element.224), channel_id=1, source_target_pairs={{0,3},{1,2},{2,1},{3,0},{4,7},{5,6},{6,5},{7,4},{8,11},{9,10},{10,... | collective-permute-start | bytes 1572872 | tf_op jit(solution)/shard_map/cond/branch_2_fun/ppermute | solution.py:35
  28.5 28.3 %collective-permute-start.13 = (bf16[2,16,32,128]{3,2,1,0:T(8,128)(2,1)S(1)}, bf16[2,16,32,128]{3,2,1,0:T(8,128)(2,1)}, u32[]{:S(2)}, u32[]{:S(2)}) collective-permute-start(bf16[2,16,32,128]{3,2,1,0:T(8,128)(2,1)S(1)} %get-tuple-element.221), channel_id=1, source_target_pairs={{0,1},{1,0},{2,3},{3,2},{4,5},{5,4},{6,7},{7,6},{8,9},{9,8},{10,11... | collective-permute-start | bytes 786440 | tf_op jit(solution)/shard_map/cond/branch_2_fun/ppermute | solution.py:35
  30.6 29.5 %collective-permute-start.15 = (bf16[2,16,32,128]{3,2,1,0:T(8,128)(2,1)}, bf16[2,16,32,128]{3,2,1,0:T(8,128)(2,1)}, u32[]{:S(2)}, u32[]{:S(2)}) collective-permute-start(bf16[2,16,32,128]{3,2,1,0:T(8,128)(2,1)} %get-tuple-element.223), channel_id=1, source_target_pairs={{0,2},{1,3},{2,0},{3,1},{4,6},{5,7},{6,4},{7,5},{8,10},{9,11},{10,... | collective-permute-start | bytes 786440 | tf_op jit(solution)/shard_map/cond/branch_2_fun/ppermute | solution.py:35
  56.9 10.1 %collective-permute-start.17 = (bf16[2,16,32,128]{3,2,1,0:T(8,128)(2,1)}, bf16[2,16,32,128]{3,2,1,0:T(8,128)(2,1)}, u32[]{:S(2)}, u32[]{:S(2)}) collective-permute-start(bf16[2,16,32,128]{3,2,1,0:T(8,128)(2,1)} %get-tuple-element.225), channel_id=1, source_target_pairs={{0,3},{1,2},{2,1},{3,0},{4,7},{5,6},{6,5},{7,4},{8,11},{9,10},{10,... | collective-permute-start | bytes 786440 | tf_op jit(solution)/shard_map/cond/branch_2_fun/ppermute | solution.py:35
  76.3 23.0 %copy-start.2 = (bf16[1,64,256,256]{3,2,1,0:T(8,128)(2,1)S(1)}, bf16[1,64,256,256]{3,2,1,0:T(8,128)(2,1)}, u32[]{:S(2)}) copy-start(bf16[1,64,256,256]{3,2,1,0:T(8,128)(2,1)} %param.13) | copy-start | bytes 25165828
  88.3 18.1 %copy-start = (bf16[64,256,256]{2,1,0:T(8,128)(2,1)}, bf16[64,256,256]{2,1,0:T(8,128)(2,1)S(1)}, u32[]{:S(2)}) copy-start(bf16[64,256,256]{2,1,0:T(8,128)(2,1)S(1)} %get-tuple-element.393.mats) | copy-start | bytes 25165828
  88.4 5.0 %collective-permute-start.85 = (bf16[256,256]{1,0:T(8,128)(2,1)S(1)}, bf16[256,256]{1,0:T(8,128)(2,1)S(1)}, u32[]{:S(2)}, u32[]{:S(2)}) collective-permute-start(bf16[256,256]{1,0:T(8,128)(2,1)S(1)} %convert_element_type.33), channel_id=1, source_target_pairs={{0,1},{1,0},{2,3},{3,2},{4,5},{5,4},{6,7},{7,6},{8,9},{9,8},{10,11... | collective-permute-start | bytes 393224 | tf_op jit(solution)/shard_map/ppermute | solution.py:35
  89.3 5.0 %collective-permute-start.86 = (bf16[256,256]{1,0:T(8,128)(2,1)S(1)}, bf16[256,256]{1,0:T(8,128)(2,1)S(1)}, u32[]{:S(2)}, u32[]{:S(2)}) collective-permute-start(bf16[256,256]{1,0:T(8,128)(2,1)S(1)} %convert_element_type.33), channel_id=1, source_target_pairs={{0,2},{1,3},{2,0},{3,1},{4,6},{5,7},{6,4},{7,5},{8,10},{9,11},{10,... | collective-permute-start | bytes 393224 | tf_op jit(solution)/shard_map/ppermute | solution.py:35
  90.7 8.4 %collective-permute-start.87 = (bf16[256,256]{1,0:T(8,128)(2,1)S(1)}, bf16[256,256]{1,0:T(8,128)(2,1)S(1)}, u32[]{:S(2)}, u32[]{:S(2)}) collective-permute-start(bf16[256,256]{1,0:T(8,128)(2,1)S(1)} %convert_element_type.33), channel_id=1, source_target_pairs={{0,3},{1,2},{2,1},{3,0},{4,7},{5,6},{6,5},{7,4},{8,11},{9,10},{10,... | collective-permute-start | bytes 393224 | tf_op jit(solution)/shard_map/ppermute | solution.py:35
  99.2 7.3 %collective-permute-start.88 = (bf16[256,256]{1,0:T(8,128)(2,1)S(1)}, bf16[256,256]{1,0:T(8,128)(2,1)S(1)}, u32[]{:S(2)}, u32[]{:S(2)}) collective-permute-start(bf16[256,256]{1,0:T(8,128)(2,1)S(1)} %add_convert_fusion.1.op), channel_id=1, source_target_pairs={{0,8},{4,12},{8,16},{12,20},{16,24},{20,28},{24,0},{28,4},{1,9},{5... | collective-permute-start | bytes 393224 | tf_op jit(solution)/shard_map/ppermute | solution.py:30
  112.1 6.1 %collective-permute-start.89 = (bf16[256,256]{1,0:T(8,128)(2,1)S(1)}, bf16[256,256]{1,0:T(8,128)(2,1)S(1)}, u32[]{:S(2)}, u32[]{:S(2)}) collective-permute-start(bf16[256,256]{1,0:T(8,128)(2,1)S(1)} %convert_element_type.38), channel_id=1, source_target_pairs={{0,1},{1,0},{2,3},{3,2},{4,5},{5,4},{6,7},{7,6},{8,9},{9,8},{10,11... | collective-permute-start | bytes 393224 | tf_op jit(solution)/shard_map/ppermute | solution.py:35
  112.5 7.8 %collective-permute-start.90 = (bf16[256,256]{1,0:T(8,128)(2,1)S(1)}, bf16[256,256]{1,0:T(8,128)(2,1)S(1)}, u32[]{:S(2)}, u32[]{:S(2)}) collective-permute-start(bf16[256,256]{1,0:T(8,128)(2,1)S(1)} %convert_element_type.38), channel_id=1, source_target_pairs={{0,2},{1,3},{2,0},{3,1},{4,6},{5,7},{6,4},{7,5},{8,10},{9,11},{10,... | collective-permute-start | bytes 393224 | tf_op jit(solution)/shard_map/ppermute | solution.py:35
  114.2 6.0 %collective-permute-start.91 = (bf16[256,256]{1,0:T(8,128)(2,1)S(1)}, bf16[256,256]{1,0:T(8,128)(2,1)S(1)}, u32[]{:S(2)}, u32[]{:S(2)}) collective-permute-start(bf16[256,256]{1,0:T(8,128)(2,1)S(1)} %convert_element_type.38), channel_id=1, source_target_pairs={{0,3},{1,2},{2,1},{3,0},{4,7},{5,6},{6,5},{7,4},{8,11},{9,10},{10,... | collective-permute-start | bytes 393224 | tf_op jit(solution)/shard_map/ppermute | solution.py:35
  120.3 5.9 %collective-permute-start.92 = (bf16[256,256]{1,0:T(8,128)(2,1)S(1)}, bf16[256,256]{1,0:T(8,128)(2,1)S(1)}, u32[]{:S(2)}, u32[]{:S(2)}) collective-permute-start(bf16[256,256]{1,0:T(8,128)(2,1)S(1)} %add_convert_fusion.op), channel_id=1, source_target_pairs={{0,16},{4,20},{8,24},{12,28},{16,0},{20,4},{24,8},{28,12},{1,17},{... | collective-permute-start | bytes 393224 | tf_op jit(solution)/shard_map/ppermute | solution.py:30
  126.3 3.4 %copy-start.1 = (bf16[64,256,256]{2,1,0:T(8,128)(2,1)S(1)}, bf16[64,256,256]{2,1,0:T(8,128)(2,1)}, u32[]{:S(2)}) copy-start(bf16[64,256,256]{2,1,0:T(8,128)(2,1)} %copy-done) | copy-start | bytes 25165828
  135.5 4.4 %collective-permute-start.93 = (f32[64,256]{1,0:T(8,128)S(1)}, f32[64,256]{1,0:T(8,128)S(1)}, u32[]{:S(2)}, u32[]{:S(2)}) collective-permute-start(f32[64,256]{1,0:T(8,128)S(1)} %get-tuple-element.422), channel_id=1, source_target_pairs={{0,1},{1,0},{2,3},{3,2},{4,5},{5,4},{6,7},{7,6},{8,9},{9,8},{10,11... | collective-permute-start | bytes 196616 | tf_op jit(solution)/shard_map/ppermute | solution.py:35
  136.7 4.3 %collective-permute-start.94 = (f32[64,256]{1,0:T(8,128)S(1)}, f32[64,256]{1,0:T(8,128)S(1)}, u32[]{:S(2)}, u32[]{:S(2)}) collective-permute-start(f32[64,256]{1,0:T(8,128)S(1)} %get-tuple-element.424), channel_id=1, source_target_pairs={{0,2},{1,3},{2,0},{3,1},{4,6},{5,7},{6,4},{7,5},{8,10},{9,11},{10,... | collective-permute-start | bytes 196616 | tf_op jit(solution)/shard_map/ppermute | solution.py:35
  137.4 5.2 %collective-permute-start.95 = (f32[64,256]{1,0:T(8,128)S(1)}, f32[64,256]{1,0:T(8,128)S(1)}, u32[]{:S(2)}, u32[]{:S(2)}) collective-permute-start(f32[64,256]{1,0:T(8,128)S(1)} %get-tuple-element.423), channel_id=1, source_target_pairs={{0,3},{1,2},{2,1},{3,0},{4,7},{5,6},{6,5},{7,4},{8,11},{9,10},{10,... | collective-permute-start | bytes 196616 | tf_op jit(solution)/shard_map/ppermute | solution.py:35
